TPU v7x, 512 devices: a whole 4x4x16 slice. The times are simulated.
512 devices in a mesh: tp: 8 (over z_hi, core), dp: 64 (over x, y, z_lo).
Axes of the slice: x: 4, y: 4, z: 16 (z_hi: 4, z_lo: 4; z = z_hi * 4 + z_lo), core: 2. Of those that a mesh axis runs over, the one named last changes fastest.
Arguments:
- context: bfloat16 [16384, 4096], P('dp', 'tp'), may hold values from -6 to 6
- stream: bfloat16 [16384, 4096], P('dp'), may hold values from -16 to 16
- w_attn_out: bfloat16 [4096, 4096], P('tp', 'dp'), may hold values from -0.09375 to 0.09375
- modulation: float32 [64, 3, 4096], P('dp'), may hold values from -3 to 3
- w_teacher_head: bfloat16 [4096, 128], P('dp'), may hold values from -0.09375 to 0.09375
- noisy: bfloat16 [16384, 128], P('dp'), may hold values from -6 to 6
- timestep: int32 [64], P('dp'), may hold values from 0 to 999
- frames: int32 [64], P('dp'), may hold values from 1 to 256, as said below
- w_in: bfloat16 [128, 2048], replicated, may hold values from -0.5 to 0.5
- w_time: bfloat16 [128, 2048], replicated, may hold values from -0.5 to 0.5
- w_up: bfloat16 [2048, 3072], P('dp', 'tp'), may hold values from -0.125 to 0.125
- w_down: bfloat16 [3072, 2048], P('tp', 'dp'), may hold values from -0.109375 to 0.109375
- w_out: bfloat16 [2048, 128], P('dp'), may hold values from -0.125 to 0.125
Outputs:
- target: float32 [16384, 128], P('dp')
- loss: float32 [], replicated
- grad_up: float32 [2048, 3072], P('dp', 'tp')
Inputs may be any that keep to these rules, and one draw needn't show every extreme that they name: The live frames of a clip are its first frames; some clip has all 256 live.
All inputs are finite; a program needn't handle non-finite values.
Results may differ from a plain program's by a relative error of at most 0.0085.
Values may be sent and summed in bfloat16 or wider, within the bound.
A program may use at most 64 MiB of HBM per device.

v0:
```python
import math

import jax
import jax.numpy as jnp
from jax import lax
from jax.sharding import PartitionSpec as P

C = 128
FREQ = 128
STEPS = 1000


loss_scale = 32768.0
norm_eps = 1e-06


def time_features(timestep):
    half = FREQ // 2
    freq_index = jnp.arange(half, dtype=jnp.float32)
    rates = jnp.exp(-math.log(10000.0) * freq_index / half)
    angles = timestep.astype(jnp.float32)[:, None] * rates[None, :]
    return jnp.concatenate([jnp.sin(angles), jnp.cos(angles)], axis=1).astype(jnp.bfloat16)


def noise_level(timestep):
    phase = (timestep.astype(jnp.float32) / STEPS + 0.008) / 1.008 * (math.pi / 2)
    return (jnp.cos(phase), jnp.sin(phase))


def gelu_slope(pre):
    inner_coef = math.sqrt(2.0 / math.pi)
    tangent = jnp.tanh(inner_coef * (pre + 0.044715 * pre * pre * pre))
    return 0.5 * (1.0 + tangent) + 0.5 * pre * (1.0 - tangent * tangent) * inner_coef * (
        1.0 + 3.0 * 0.044715 * pre * pre
    )


def local(
    context,
    stream,
    w_attn_out,
    modulation,
    w_teacher_head,
    noisy,
    timestep,
    frames,
    w_in,
    w_time,
    w_up,
    w_down,
    w_out,
):
    partial_attn = jnp.dot(
        context,
        lax.all_gather(w_attn_out, "dp", axis=1, tiled=True),
        preferred_element_type=jnp.float32,
    )
    whole_head = lax.all_gather(w_teacher_head, "dp", axis=0, tiled=True)
    modulate = modulation[0]
    attention = lax.psum(partial_attn.astype(jnp.bfloat16), "tp").astype(jnp.float32)
    state = stream.astype(jnp.float32) + modulate[0][None, :] * attention
    center = jnp.mean(state, axis=-1, keepdims=True)
    spread = jnp.mean((state - center) ** 2, axis=-1, keepdims=True)
    normed = (state - center) * lax.rsqrt(spread + norm_eps) * (
        1.0 + modulate[2][None, :]
    ) + modulate[1][None, :]
    velocity = jnp.dot(normed.astype(jnp.bfloat16), whole_head, preferred_element_type=jnp.float32)
    signal, noise = noise_level(timestep)
    target = signal[0] * velocity + noise[0] * noisy.astype(jnp.float32)
    features = time_features(timestep)
    time_row = jnp.dot(features, w_time, preferred_element_type=jnp.float32)
    lifted_f = jnp.dot(noisy, w_in, preferred_element_type=jnp.float32) + time_row
    lifted = jax.nn.silu(lifted_f).astype(jnp.bfloat16)
    columns = lifted
    pre = jnp.dot(
        columns, lax.all_gather(w_up, "dp", axis=0, tiled=True), preferred_element_type=jnp.float32
    )
    down_whole = lax.all_gather(w_down, "dp", axis=1, tiled=True)
    out_whole = lax.all_gather(w_out, "dp", axis=0, tiled=True)
    hidden = jax.nn.gelu(pre, approximate=True).astype(jnp.bfloat16)
    down = lax.psum(
        jnp.dot(hidden, down_whole, preferred_element_type=jnp.float32).astype(jnp.bfloat16), "tp"
    ).astype(jnp.float32)
    mixed = lifted_f + down
    inv_rms = lax.rsqrt(jnp.mean(mixed * mixed, axis=-1, keepdims=True) + norm_eps)
    unit = mixed * inv_rms
    pred = jnp.dot(unit.astype(jnp.bfloat16), out_whole, preferred_element_type=jnp.float32)
    live = (jnp.arange(noisy.shape[0], dtype=jnp.int32) < frames[0]).astype(jnp.float32)[:, None]
    error = pred - target
    error_total, count = lax.psum(
        (jnp.sum(live * error * error), jnp.sum(frames.astype(jnp.float32))), "dp"
    )
    loss = error_total / (count * C)
    grad_pred = (loss_scale * 2.0 / (count * C) * live * error).astype(jnp.bfloat16)
    grad_unit = jnp.dot(grad_pred, out_whole.T, preferred_element_type=jnp.float32)
    grad_mixed = inv_rms * (grad_unit - unit * jnp.mean(grad_unit * unit, axis=-1, keepdims=True))
    grad_mixed = grad_mixed.astype(jnp.bfloat16)
    grad_hidden = jnp.dot(grad_mixed, down_whole.T, preferred_element_type=jnp.float32)
    grad_pre = (grad_hidden * gelu_slope(pre)).astype(jnp.bfloat16)
    columns = lifted
    grad_up = lax.psum_scatter(
        lax.dot_general(
            columns, grad_pre, (((0,), (0,)), ((), ())), preferred_element_type=jnp.float32
        ),
        "dp",
        scatter_dimension=0,
        tiled=True,
    )
    return (target, loss, grad_up)


def solution(mesh):
    in_specs = (
        P("dp", "tp"),
        P("dp", None),
        P("tp", "dp"),
        P("dp", None, None),
        P("dp", None),
        P("dp", None),
        P("dp"),
        P("dp"),
        P(),
        P(),
        P("dp", "tp"),
        P("tp", "dp"),
        P("dp", None),
    )
    out_specs = (P("dp", None), P(), P("dp", "tp"))
    return jax.shard_map(local, mesh=mesh, in_specs=in_specs, out_specs=out_specs, check_vma=False)
```

profile of v0, /device:TPU:128, one launch (start us, length us, event | category | flops | bytes accessed | tf_op | source)
XLA Modules:
  0.0 2209.4 jit_solution(2146005477533302199)
XLA Ops:
  7.2 0.7 all-gather.9.cloned.1.call-update
  7.9 0.0 all-gather.11.cloned.1.call-start
  8.0 0.7 all-gather.11.cloned.1.call-update
  8.7 0.0 all-gather.5.cloned.1.call-start
  8.7 0.7 all-gather.5.cloned.1.call-update
  9.4 0.0 all-reduce.4.cloned.1.call-start
  10.1 0.1 cosine_convert_fusion
  10.1 1.3 fusion.48
  11.4 1.3 convolution_add_fusion
  12.7 354.5 %all-gather.9.cloned.1.call-done = bf16[2048,384]{1,0:T(8,128)(2,1)} async-done(((bf16[32,384]{1,0:T(8,128)(2,1)}), bf16[2048,384]{1,0:T(8,128)(2,1)}) %all-gather.9.cloned.1.call-update) | async-done | bytes 1572880 | tf_op jit(solution)/shard_map/all_gather | solution.py:76
  367.2 2.1 fusion.61
  369.4 351.6 %all-gather.11.cloned.1.call-done = bf16[384,2048]{0,1:T(8,128)(2,1)} async-done(((bf16[384,32]{0,1:T(8,128)(2,1)}), bf16[384,2048]{0,1:T(8,128)(2,1)}) %all-gather.11.cloned.1.call-update) | async-done | bytes 1572880 | tf_op jit(solution)/shard_map/all_gather | solution.py:78
  720.9 3.1 convolution_convert_fusion.1
  724.1 359.8 %all-gather.5.cloned.1.call-done = bf16[512,4096]{0,1:T(8,128)(2,1)} async-done(((bf16[512,64]{0,1:T(8,128)(2,1)}), bf16[512,4096]{0,1:T(8,128)(2,1)}) %all-gather.5.cloned.1.call-update) | async-done | bytes 4194320 | tf_op jit(solution)/shard_map/all_gather | solution.py:55
  1083.9 4.8 convolution_convert_fusion
  1088.7 0.0 all-gather.7.cloned.1.call-start
  1088.8 0.5 all-gather.7.cloned.1.call-update
  1089.3 0.0 reduce-scatter.2.cloned.1.call-start
  1089.4 0.1 copy-done.9
  1090.4 225.8 %all_gather.19 = bf16[2048,128]{1,0:T(8,128)(2,1)S(1)} all-gather(bf16[32,128]{1,0:T(8,128)(2,1)S(1)} %copy-done.10), channel_id=1, replica_groups=mesh['tp'=8,'dp'=64] {'dp'}, dimensions={0}, use_global_device_ids=true | all-gather | bytes 532480 | tf_op jit(solution)/shard_map/all_gather | solution.py:79
  1316.2 3.1 fusion
  1319.3 0.3 copy-done.4
  1319.7 1.1 multiply_reduce_fusion
  1320.8 0.1 copy-done.1
  1320.9 0.4 multiply_reduce_fusion.2
  1321.3 296.6 %all-gather.7.cloned.1.call-done = bf16[4096,128]{1,0:T(8,128)(2,1)} async-done(((bf16[64,128]{1,0:T(8,128)(2,1)}), bf16[4096,128]{1,0:T(8,128)(2,1)}) %all-gather.7.cloned.1.call-update) | async-done | bytes 1048592 | tf_op jit(solution)/shard_map/all_gather | solution.py:58
  1617.9 4.0 fusion.5
  1621.9 1.1 fusion.43
  1623.1 189.4 %all-reduce = (f32[]{:T(128)}, f32[]{:T(128)}) all-reduce(f32[]{:T(128)} %get-tuple-element.10, f32[]{:T(128)} %bitcast.9), channel_id=1, replica_groups=mesh['tp'=8,'dp'=64] {'dp'}, use_global_device_ids=true, to_apply=%region_6.7 | all-reduce | flops 2 | bytes 16 | tf_op jit(solution)/shard_map/psum | solution.py:90
  1813.2 3.1 multiply_reduce_fusion.1
  1816.3 5.7 fusion.3
  1822.7 378.7 %reduce-scatter.2.cloned.1.call-done = f32[32,384]{1,0:T(8,128)} async-done(((f32[2048,384]{1,0:T(8,128)}), f32[32,384]{1,0:T(8,128)}) %reduce-scatter.2.cloned.1.call-update) | async-done | bytes 49168 | tf_op jit(solution)/shard_map/reduce_scatter | solution.py:101
  (30 shorter events, 0.2 us)
Async XLA Ops:
  7.2 4.3 copy-start
  7.2 360.0 %all-gather.9.cloned.1.call-start = ((), (), s32[]{:S(2)}) async-start(), calls=%async_computation.3 | async-start | bytes 1597440 | tf_op jit(solution)/shard_map/all_gather | solution.py:76
  7.9 713.0 %all-gather.11.cloned.1.call-start = ((), (), s32[]{:S(2)}) async-start(), calls=%async_computation.4 | async-start | bytes 1597440 | tf_op jit(solution)/shard_map/all_gather | solution.py:78
  8.7 1075.2 %all-gather.5.cloned.1.call-start = ((), (), s32[]{:S(2)}) async-start(), calls=%async_computation.1 | async-start | bytes 4259840 | tf_op jit(solution)/shard_map/all_gather | solution.py:55
  9.4 1306.8 %all-reduce.4.cloned.1.call-start = ((), (), s32[]{:S(2)}) async-start(), calls=%async_computation.6 | async-start | bytes 6291456 | tf_op jit(solution)/shard_map/psum | solution.py:60
  369.3 719.4 %copy-start.5 = (f32[256,384]{1,0:T(8,128)}, f32[256,384]{1,0:T(8,128)S(1)}, u32[]{:S(2)}) copy-start(f32[256,384]{1,0:T(8,128)S(1)} %fusion.61) | copy-start | bytes 1179652
  369.3 714.6 %copy-start.6 = (bf16[256,512]{1,0:T(8,128)(2,1)S(1)}, bf16[256,512]{1,0:T(8,128)(2,1)}, u32[]{:S(2)}) copy-start(bf16[256,512]{1,0:T(8,128)(2,1)} %param.13) | copy-start | bytes 786436
  1088.7 0.8 copy-start.9
  1088.7 1.6 copy-start.10
  1088.7 529.2 %all-gather.7.cloned.1.call-start = ((), (), s32[]{:S(2)}) async-start(), calls=%async_computation.2 | async-start | bytes 1064960 | tf_op jit(solution)/shard_map/all_gather | solution.py:58
  1089.3 1112.0 %reduce-scatter.2.cloned.1.call-start = ((), (), s32[]{:S(2)}) async-start(), calls=%async_computation.5 | async-start | bytes 3194880 | tf_op jit(solution)/shard_map/reduce_scatter | solution.py:101
  1316.2 3.2 copy-start.3
  1316.2 3.5 copy-start.4
  1319.7 1.2 copy-start.1
  1320.8 297.2 %copy-start.8 = (bf16[256,128]{1,0:T(8,128)(2,1)S(1)}, bf16[256,128]{1,0:T(8,128)(2,1)}, u32[]{:S(2)}) copy-start(bf16[256,128]{1,0:T(8,128)(2,1)} %param.18) | copy-start | bytes 196612
  1617.9 4.0 copy-start.2
  1621.9 194.3 %copy-start.7 = (f32[256,128]{1,0:T(8,128)}, f32[256,128]{1,0:T(8,128)S(1)}, u32[]{:S(2)}) copy-start(f32[256,128]{1,0:T(8,128)S(1)} %fusion.5) | copy-start | bytes 393220
Sparse Core Ops, SparseCore 0:
  10.1 357.0 all-gather.8
  369.3 351.5 all-gather.10
  723.0 360.8 all-gather.4
  1088.9 171.1 all-reduce.3
  1262.0 355.8 all-gather.6
  1822.2 379.1 reduce-scatter.1
where the time goes:
time: 2210 us
  waiting for transfers between devices  1740 us (79%)
  blocking collectives  415 us (19%)
  matrix products  26.5 us (1%)
    reduce_scatter x1, waiting for transfers between devices, local(): lax.psum_scatter(lax.dot_general(columns, grad_pre, (((0,), (0,)), ((), (...  379 us
    all_gather x1, waiting for transfers between devices, local(): lax.all_gather(w_attn_out, 'dp', axis=1, tiled=True)  360 us
    all_gather x1, waiting for transfers between devices, local(): lax.all_gather(w_up, 'dp', axis=0, tiled=True)  355 us
    all_gather x1, waiting for transfers between devices, local(): down_whole = lax.all_gather(w_down, 'dp', axis=1, tiled=True)  352 us
    all_gather x1, waiting for transfers between devices, local(): whole_head = lax.all_gather(w_teacher_head, 'dp', axis=0, tiled=True)  297 us
    all_gather x1, blocking collectives, local(): out_whole = lax.all_gather(w_out, 'dp', axis=0, tiled=True)  226 us
    psum x1, blocking collectives, local(): lax.psum((jnp.sum(live * error * error), jnp.sum(frames.astype(jnp.float3...  189 us
  transfers between devices with their start and end apart: 6, of which 5 were waited for; matrix products, arithmetic and copies ran while one was open for 1% of the time, Pallas kernels for 0%

commit v1 on v0

v1 whole, which is shorter than its diff:
```python
import math

import jax
import jax.numpy as jnp
from jax import lax
from jax.experimental import pallas as pl
from jax.experimental.pallas import tpu as pltpu
from jax.sharding import PartitionSpec as P

C = 128
FREQ = 128
STEPS = 1000
LOSS_SCALE = 32768.0
EPS = 1e-06
F32 = jnp.float32
BF16 = jnp.bfloat16
MESH = pl.DeviceIdType.MESH
N_SEND = 520

COUNTS = dict(
    ctx=8, ag=128, ring=36, sib=32, sp=16, st=16, mod=16, head=4, nf=16, wo1=4, wo2=16, cnt=4,
    dn=16, un=32, tm=16, gp=16, lx=16, tg=8, lt=8, lz=4, g1=4, g2=4, g3=4, g4=16,
)
BASE = {}
N_RECV = 0
for _name, _count in COUNTS.items():
    BASE[_name] = N_RECV
    N_RECV += _count

XY = [(dx, dy) for dx in range(4) for dy in range(4) if dx or dy]


def dot_nt(a, b):
    return lax.dot_general(a, b, (((1,), (1,)), ((), ())), preferred_element_type=F32)


def dot_nn(a, b):
    return jnp.dot(a, b, preferred_element_type=F32)


def dot_tn(a, b):
    return lax.dot_general(a, b, (((0,), (0,)), ((), ())), preferred_element_type=F32)


def split_dot(a, b):
    high = a.astype(BF16)
    low = (a - high.astype(F32)).astype(BF16)
    return dot_nn(high, b) + dot_nn(low, b)


def body(
    ctx, wt, sp, stream, mod, head, nf, info, wo, wit,
    tgt_out, grad_out, loss_out,
    ctxp, w4, s4, srecv, strb, modb, headb, nfb, woutb, lifted, slope, hidden, dnsend, dnrecv,
    unitb, ubuf, gbuf, att, zbuf, tsend, trecv, gpb, tgb, g1, r1, g2, r2, g3, r3, g4s, g4r,
    lx, lt, lz, cz, send_sem, recv_sem,
):
    tp = lax.axis_index("tp")
    dp = lax.axis_index("dp")
    zh, c = lax.div(tp, 2), lax.rem(tp, 2)
    xy, zl = lax.div(dp, 4), lax.rem(dp, 4)
    x, y = lax.div(xy, 4), lax.rem(xy, 4)
    z = zh * 4 + zl
    sibling = zh * 2 + (1 - c)

    def plane(dx, dy):
        return lax.rem(x + dx, 4) * 4 + lax.rem(y + dy, 4)

    def other(v, d):
        return lax.rem(v + d, 4)

    barrier = pltpu.get_barrier_semaphore()
    partners = [(tp, plane(dx, dy) * 4 + zl) for dx, dy in XY]
    partners += [(lax.rem(tp + d, 8), dp) for d in range(1, 8)]
    for step in (1, 15):
        zz = lax.rem(z + step, 16)
        partners.append((lax.div(zz, 4) * 2 + c, xy * 4 + lax.rem(zz, 4)))
    partners += [(tp, xy * 4 + other(zl, d)) for d in (1, 2, 3)]
    for p_tp, p_dp in partners:
        pl.semaphore_signal(barrier, inc=1, device_id={"tp": p_tp, "dp": p_dp}, device_id_type=MESH)
    pl.semaphore_wait(barrier, len(partners))

    sends = []

    def send(src, dst, kind, index, to_tp, to_dp):
        copy = pltpu.make_async_remote_copy(
            src_ref=src, dst_ref=dst,
            send_sem=send_sem.at[len(sends)], recv_sem=recv_sem.at[BASE[kind] + index],
            device_id={"tp": to_tp, "dp": to_dp}, device_id_type=MESH,
        )
        copy.start()
        sends.append(copy)

    def arrived(dst, kind, index):
        pltpu.make_async_remote_copy(
            src_ref=dst, dst_ref=dst,
            send_sem=send_sem.at[0], recv_sem=recv_sem.at[BASE[kind] + index],
            device_id={"tp": tp, "dp": dp}, device_id_type=MESH,
        ).wait_recv()

    def to_plane(source, target, kind):
        for dx, dy in XY:
            p = plane(dx, dy)
            send(source(p), target.at[xy], kind, xy, tp, p * 4 + zl)

    def from_plane(target, kind):
        for dx, dy in XY:
            p = plane(dx, dy)
            arrived(target.at[p], kind, p)

    def gather_own(view, kind, base):
        for d in (1, 3, 2):
            px, py = other(x, d) * 4 + y, x * 4 + other(y, d)
            send(view(xy, None), view(xy, None), kind, base + xy * 2, tp, px * 4 + zl)
            send(view(xy, None), view(xy, None), kind, base + xy * 2, tp, py * 4 + zl)

    def gather_forward(view, kind, base):
        for d in (1, 3, 2):
            px, py = other(x, d) * 4 + y, x * 4 + other(y, d)
            arrived(view(px, None), kind, base + px * 2)
            for e in (1, 3, 2):
                send(view(px, 0), view(px, 0), kind, base + px * 2, tp, (x * 4 + other(y, e)) * 4 + zl)
            arrived(view(py, None), kind, base + py * 2)
            for e in (1, 3, 2):
                send(view(py, 1), view(py, 1), kind, base + py * 2 + 1, tp, (other(x, e) * 4 + y) * 4 + zl)

    def gather_last(view, kind, base):
        for dx in (1, 2, 3):
            for dy in (1, 2, 3):
                p = plane(dx, dy)
                arrived(view(p, 0), kind, base + p * 2)
                arrived(view(p, 1), kind, base + p * 2 + 1)

    def ctx_view(chunk):
        def view(source, half):
            if half is None:
                return ctxp.at[pl.ds(2 * chunk, 2), source]
            return ctxp.at[pl.ds(2 * chunk, 2), source, pl.ds(16 * half, 16)]

        return view

    def unit_view(source, half):
        if half is None:
            return unitb.at[source]
        return unitb.at[source, pl.ds(16 * half, 16)]

    def slot(kind, zz, core):
        if kind == 0:
            return w4.at[lax.div(zz, 4) * 2 + core, lax.rem(zz, 4)]
        return s4.at[core, lax.div(zz, 4), lax.rem(zz, 4)]

    def ring_send(kind, zz, hop, direction):
        to = lax.rem(z + (1 if direction == 0 else 15), 16)
        ref = slot(kind, zz, c)
        send(ref, ref, "ring", (kind * 2 + direction) * 9 + hop,
             lax.div(to, 4) * 2 + c, xy * 4 + lax.rem(to, 4))

    def sibling_send(kind, zz):
        ref = slot(kind, zz, c)
        send(ref, ref, "sib", kind * 16 + zz, sibling, dp)

    def ring_start(kind):
        ring_send(kind, z, 1, 0)
        ring_send(kind, z, 1, 1)
        sibling_send(kind, z)

    def ring_step(kind, hop):
        for direction, last in ((0, 8), (1, 7)):
            if hop > last:
                continue
            zz = lax.rem(z + (16 - hop if direction == 0 else hop), 16)
            arrived(slot(kind, zz, c), "ring", (kind * 2 + direction) * 9 + hop)
            if hop < last:
                ring_send(kind, zz, hop + 1, direction)
            sibling_send(kind, zz)

    def ring_last(kind):
        for zz in range(16):
            arrived(slot(kind, zz, 1 - c), "sib", kind * 16 + zz)

    ctxp[tp, xy] = ctx[tp]
    for d in (1, 2, 7, 6, 3, 5, 4):
        t = lax.rem(tp + d, 8)
        send(ctx.at[t], ctxp.at[tp, xy], "ctx", tp, t, dp)
    to_plane(lambda p: sp.at[p], srecv, "sp")
    srecv[xy] = sp[xy]
    w4[tp, zl] = wt[...]
    ring_start(0)
    nfb[xy] = nf[tp]
    to_plane(lambda p: nf.at[tp], nfb, "nf")
    woutb[zl, xy] = wo[...]
    headb[zl] = head[...]
    for d in (1, 2, 3):
        other_dp = xy * 4 + other(zl, d)
        send(wo, woutb.at[zl, xy], "wo1", zl, tp, other_dp)
        send(head, headb.at[zl], "head", zl, tp, other_dp)
    modb[xy] = mod[:, pl.ds(pl.multiple_of(xy * 256, 256), 256)]
    to_plane(lambda p: mod.at[:, pl.ds(pl.multiple_of(p * 256, 256), 256)], modb, "mod")
    rows = pl.ds(pl.multiple_of(tp * 32, 32), 32)
    own_stream = pltpu.make_async_copy(
        stream.at[rows, pl.ds(pl.multiple_of(xy * 256, 256), 256)], strb.at[xy], send_sem.at[N_SEND - 1]
    )
    own_stream.start()
    to_plane(lambda p: stream.at[rows, pl.ds(pl.multiple_of(p * 256, 256), 256)], strb, "st")

    def ctx_own(chunk_step):
        chunk = other(zh, chunk_step)
        if chunk_step == 0:
            arrived(ctxp.at[sibling, xy], "ctx", sibling)
        else:
            arrived(ctxp.at[2 * chunk, xy], "ctx", 2 * chunk)
            arrived(ctxp.at[2 * chunk + 1, xy], "ctx", 2 * chunk + 1)
        gather_own(ctx_view(chunk), "ag", chunk * 32)

    def ctx_forward(chunk_step):
        chunk = other(zh, chunk_step)
        gather_forward(ctx_view(chunk), "ag", chunk * 32)

    group = lax.div(lax.broadcasted_iota(jnp.int32, (16, 128), 1), 32)
    from_plane(srecv, "sp")
    for t in range(4):
        pieces = [srecv[4 * t + g].astype(F32) for g in range(4)]
        for q in range(4):
            tile = jnp.zeros((16, 128), F32)
            for g in range(4):
                shift = ((g - q) * 32) % 128
                moved = pltpu.roll(pieces[g], shift, 1) if shift else pieces[g]
                tile = jnp.where(group == g, moved, tile)
            hidden[8 * q : 8 * q + 8, 128 * t : 128 * t + 128] = tile[0:8]
            hidden[32 + 8 * q : 40 + 8 * q, 128 * t : 128 * t + 128] = tile[8:16]
    s4[c, zh, zl] = hidden[0:64, 0:512].astype(BF16)
    ring_start(1)

    ctx_own(0)

    def lift(block):
        piece = nfb[4 * block : 4 * block + 4].reshape(128, 256)
        for n in range(4):
            v = dot_nn(piece, wit[:, 512 * n : 512 * n + 512])
            v = v / (1.0 + jnp.exp(-v))
            lifted[128 * block : 128 * block + 128, 512 * n : 512 * n + 512] = v.astype(BF16)

    from_plane(nfb, "nf")
    ring_step(0, 1)
    ring_step(1, 1)
    lift(0)
    ctx_own(1)
    ctx_forward(0)
    ring_step(0, 2)
    ring_step(1, 2)
    lift(1)
    ctx_own(3)
    ctx_forward(1)
    for d in (1, 2, 3):
        zo = other(zl, d)
        arrived(woutb.at[zo, xy], "wo1", zo)
    for dx, dy in XY:
        p = plane(dx, dy)
        send(woutb.at[:, xy], woutb.at[:, xy], "wo2", xy, tp, p * 4 + zl)
    ring_step(0, 3)
    ring_step(1, 3)
    lift(2)
    ctx_own(2)
    ctx_forward(3)
    ring_step(0, 4)
    ring_step(1, 4)
    lift(3)
    ring_step(0, 5)
    ring_step(1, 5)
    ctx_forward(2)
    ring_step(0, 6)
    ring_step(1, 6)
    from_plane(modb, "mod")
    count_part = modb[0, 3:4, 0:128]
    for s in range(1, 16):
        count_part = count_part + modb[s, 3:4, 0:128]
    cz[zl] = jnp.broadcast_to(count_part, (8, 128))
    for d in (1, 2, 3):
        send(cz.at[zl], cz.at[zl], "cnt", zl, tp, xy * 4 + other(zl, d))
    for hop in (7, 8):
        ring_step(0, hop)
        ring_step(1, hop)
    ring_last(1)

    def up_part(zb):
        return s4[:, :, zb, 0:32, :].reshape(256, 512)

    def down_part(zb):
        return s4[:, :, zb, 32:64, :].reshape(256, 512)

    k0 = math.sqrt(2.0 / math.pi)
    for block in range(2):
        rs = slice(256 * block, 256 * block + 256)
        pre = dot_nt(lifted[rs, 0:512], up_part(0))
        for zb in range(1, 4):
            pre = pre + dot_nt(lifted[rs, 512 * zb : 512 * zb + 512], up_part(zb))
        tangent = jnp.tanh(k0 * (pre + 0.044715 * pre * pre * pre))
        slope[rs] = 0.5 * (1.0 + tangent) + 0.5 * pre * (1.0 - tangent * tangent) * k0 * (
            1.0 + 3.0 * 0.044715 * pre * pre
        )
        act = (0.5 * pre * (1.0 + tangent)).astype(BF16)
        for zb in range(4):
            part = dot_nn(act, down_part(zb)).astype(BF16)
            dnsend[8 * block : 8 * block + 8, :, 512 * zb : 512 * zb + 512] = part.reshape(8, 32, 512)
    dnrecv[xy] = dnsend[xy]
    to_plane(lambda p: dnsend.at[p], dnrecv, "dn")

    ring_last(0)
    for d in (1, 2, 3):
        zo = other(zl, d)
        arrived(headb.at[zo], "head", zo)
    from_plane(strb, "st")
    own_stream.wait()
    for step in (0, 1, 3, 2):
        gather_last(ctx_view(other(zh, step)), "ag", other(zh, step) * 32)
    att[...] = jnp.zeros_like(att)

    def att_step(t, carry):
        att[...] += dot_nt(ctxp[t].reshape(512, 512), w4[t].reshape(256, 512))
        return carry

    lax.fori_loop(0, 8, att_step, 0)
    lane = lax.broadcasted_iota(jnp.int32, (32, 128), 1)

    def norm_step(s, carry):
        state = strb[s].astype(F32) + modb[s, 0:1] * att[pl.ds(pl.multiple_of(s * 32, 32), 32)]
        center = jnp.mean(state, axis=-1, keepdims=True)
        state = state - center
        square = jnp.sum(state * state, axis=-1, keepdims=True)
        zbuf[s] = (state * (1.0 + modb[s, 2:3])).astype(BF16)
        tsend[s, 32:64] = jnp.where(lane < 64, center, square)
        return carry

    lax.fori_loop(0, 16, norm_step, 0)
    whole_head = headb[...].reshape(256, 128)
    tsend[:, 0:32] = dot_nn(zbuf[...].reshape(512, 256), whole_head).reshape(16, 32, 128)
    ones_row = (lax.broadcasted_iota(jnp.int32, (1, 8, 1), 1) == 2).astype(F32)
    vectors = (modb[...] + ones_row).reshape(128, 256)
    tsend[:, 64:72] = split_dot(vectors, whole_head).reshape(16, 8, 128)
    trecv[xy] = tsend[xy]
    to_plane(lambda p: tsend.at[p], trecv, "tm")

    from_plane(dnrecv, "dn")
    from_plane(_Columns(woutb), "wo2")
    own_nf = nf[tp]

    def down_sum(s, total):
        return total + dnrecv[s].astype(F32)

    mixed = dot_nn(own_nf, wit[...])
    mixed = lax.fori_loop(0, 16, down_sum, mixed)
    inv_rms = lax.rsqrt(jnp.mean(mixed * mixed, axis=-1, keepdims=True) + EPS)
    unit_b = (mixed * inv_rms).astype(BF16)
    unitb[xy] = unit_b
    gather_own(unit_view, "un", 0)
    whole_out = woutb[...].reshape(2048, 128)
    pred = dot_nn(unit_b, whole_out)
    gather_forward(unit_view, "un", 0)
    fold = dot_nn(down_part(0), whole_out[0:512])
    for zb in range(1, 4):
        fold = fold + dot_nn(down_part(zb), whole_out[512 * zb : 512 * zb + 512])
    gbuf[...] = fold.astype(BF16)

    for d in (1, 2, 3):
        zo = other(zl, d)
        arrived(cz.at[zo], "cnt", zo)
    count = cz[0, 0:1] + cz[1, 0:1] + cz[2, 0:1] + cz[3, 0:1]
    from_plane(trecv, "tm")
    velocity = trecv[0, 0:32]
    center = trecv[0, 32:64, 0:1]
    square = trecv[0, 32:64, 127:128]
    shift_row = trecv[0, 65:66]
    for s in range(1, 16):
        velocity = velocity + trecv[s, 0:32]
        center = center + trecv[s, 32:64, 0:1]
        square = square + trecv[s, 32:64, 127:128]
        shift_row = shift_row + trecv[s, 65:66]
    center = center * (1.0 / 16.0)
    for s in range(16):
        gap = trecv[s, 32:64, 0:1] - center
        square = square + 256.0 * gap * gap
        velocity = velocity + gap * trecv[s, 66:67]
    velocity = velocity * lax.rsqrt(square * (1.0 / 4096.0) + EPS) + shift_row
    target = info[0:1] * velocity + info[1:2] * own_nf[:, 0:128].astype(F32)
    tgb[tp] = target
    frame = (lax.broadcasted_iota(jnp.int32, (32, 128), 0) + tp * 32).astype(F32)
    live = (frame < info[2:3]).astype(F32)
    error = pred - target
    grad_pred = (LOSS_SCALE * 2.0 / (count * C)) * live * error
    along = jnp.sum(grad_pred * pred, axis=-1, keepdims=True) * (1.0 / 2048.0)
    gpb[xy, :, 0:128] = (inv_rms * grad_pred).astype(BF16)
    gpb[xy, :, 128:256] = jnp.broadcast_to(inv_rms * along, (32, 128)).astype(BF16)
    to_plane(lambda p: gpb.at[xy], gpb, "gp")
    lx[xy] = jnp.broadcast_to(jnp.sum(live * error * error), (8, 128))
    to_plane(lambda p: lx.at[xy], lx, "lx")
    for d in (1, 2, 7, 6, 3, 5, 4):
        send(tgb.at[tp], tgb.at[tp], "tg", tp, lax.rem(tp + d, 8), dp)

    gather_last(unit_view, "un", 0)
    for block in range(4):
        piece = unitb[4 * block : 4 * block + 4].reshape(128, 2048)
        along_down = dot_nt(piece[:, 0:512], down_part(0))
        for zb in range(1, 4):
            along_down = along_down + dot_nt(piece[:, 512 * zb : 512 * zb + 512], down_part(zb))
        ubuf[128 * block : 128 * block + 128] = along_down
    from_plane(gpb, "gp")
    both = gpb[...].reshape(512, 256)
    grad_hidden = dot_nt(both[:, 0:128], gbuf[...]) - both[:, 128:129].astype(F32) * ubuf[...]
    grad_pre = (grad_hidden * slope[...]).astype(BF16)
    for zb in range(4):
        g1[:, :, zb] = dot_tn(grad_pre, lifted[:, 512 * zb : 512 * zb + 512]).reshape(2, 4, 32, 512)
        send(g1.at[1 - c, :, zb], r1.at[:, zb], "g1", zb, sibling, dp)
    for zb in range(4):
        arrived(r1.at[:, zb], "g1", zb)
        g2[zb] = (g1[c, :, zb] + r1[:, zb]).astype(BF16)
    r2[zl] = g2[zl]
    for d in (1, 2, 3):
        zo = other(zl, d)
        send(g2.at[zo], r2.at[zl], "g2", zl, tp, xy * 4 + zo)
    from_plane(lx, "lx")
    loss_sum = lx[0]
    for s in range(1, 16):
        loss_sum = loss_sum + lx[s]
    lt[tp] = loss_sum
    for d in range(1, 8):
        send(lt.at[tp], lt.at[tp], "lt", tp, lax.rem(tp + d, 8), dp)
    for d in (1, 2, 3):
        zo = other(zl, d)
        arrived(r2.at[zo], "g2", zo)
    g3[...] = (r2[0].astype(F32) + r2[1].astype(F32) + r2[2].astype(F32) + r2[3].astype(F32)).astype(BF16)
    r3[zh] = g3[zh]
    for d in (1, 2, 3):
        ho = other(zh, d)
        send(g3.at[ho], r3.at[zh], "g3", zh, ho * 2 + c, dp)
    for d in range(1, 8):
        t = lax.rem(tp + d, 8)
        arrived(lt.at[t], "lt", t)
    loss_sum = lt[0]
    for s in range(1, 8):
        loss_sum = loss_sum + lt[s]
    lz[zl] = loss_sum
    for d in (1, 2, 3):
        send(lz.at[zl], lz.at[zl], "lz", zl, tp, xy * 4 + other(zl, d))
    for d in (1, 2, 3):
        ho = other(zh, d)
        arrived(r3.at[ho], "g3", ho)
    total = r3[0].astype(F32) + r3[1].astype(F32) + r3[2].astype(F32) + r3[3].astype(F32)
    group8 = lax.div(lax.broadcasted_iota(jnp.int32, (8, 128), 1), 32)
    for t in range(4):
        for g in range(4):
            tile = jnp.zeros((8, 128), F32)
            for q in range(4):
                shift = ((q - g) * 32) % 128
                piece = total[8 * q : 8 * q + 8, 128 * t : 128 * t + 128]
                moved = pltpu.roll(piece, shift, 1) if shift else piece
                tile = jnp.where(group8 == q, moved, tile)
            g4s[4 * t + g] = tile
    g4r[xy] = g4s[xy]
    to_plane(lambda p: g4s.at[p], g4r, "g4")
    for d in (1, 2, 3):
        zo = other(zl, d)
        arrived(lz.at[zo], "lz", zo)
    loss_out[...] = (lz[0] + lz[1] + lz[2] + lz[3]) / (count * C)
    for d in range(1, 8):
        t = lax.rem(tp + d, 8)
        arrived(tgb.at[t], "tg", t)
    tgt_out[...] = tgb[...]
    from_plane(g4r, "g4")
    grad_out[...] = g4r[...]
    for copy in sends:
        copy.wait_send()
    assert len(sends) < N_SEND


class _Columns:
    def __init__(self, ref):
        self.ref = ref

    @property
    def at(self):
        return self

    def __getitem__(self, p):
        return self.ref.at[:, p]


def call(*args):
    vmem = pl.BlockSpec(memory_space=pltpu.VMEM)
    hbm = pl.BlockSpec(memory_space=pl.ANY)
    V = pltpu.VMEM
    return pl.pallas_call(
        body,
        out_shape=(
            jax.ShapeDtypeStruct((8, 32, 128), F32),
            jax.ShapeDtypeStruct((16, 8, 128), F32),
            jax.ShapeDtypeStruct((8, 128), F32),
        ),
        in_specs=[vmem, vmem, vmem, hbm, vmem, vmem, vmem, vmem, vmem, vmem],
        out_specs=(vmem, vmem, vmem),
        scratch_shapes=[
            V((8, 16, 32, 512), BF16),
            V((8, 4, 64, 512), BF16),
            V((2, 4, 4, 64, 512), BF16),
            V((16, 16, 128), BF16),
            V((16, 32, 256), BF16),
            V((16, 8, 256), F32),
            V((4, 64, 128), BF16),
            V((16, 32, 256), BF16),
            V((4, 16, 32, 128), BF16),
            V((512, 2048), BF16),
            V((512, 256), F32),
            V((64, 512), F32),
            V((16, 32, 2048), BF16),
            V((16, 32, 2048), BF16),
            V((16, 32, 2048), BF16),
            V((512, 256), F32),
            V((256, 128), BF16),
            V((512, 256), F32),
            V((16, 32, 256), BF16),
            V((16, 72, 128), F32),
            V((16, 72, 128), F32),
            V((16, 32, 256), BF16),
            V((8, 32, 128), F32),
            V((2, 4, 4, 32, 512), F32),
            V((4, 4, 32, 512), F32),
            V((4, 4, 32, 512), BF16),
            V((4, 4, 32, 512), BF16),
            V((4, 32, 512), BF16),
            V((4, 32, 512), BF16),
            V((16, 8, 128), F32),
            V((16, 8, 128), F32),
            V((16, 8, 128), F32),
            V((8, 8, 128), F32),
            V((4, 8, 128), F32),
            V((4, 8, 128), F32),
            pltpu.SemaphoreType.DMA((N_SEND,)),
            pltpu.SemaphoreType.DMA((N_RECV,)),
        ],
        compiler_params=pltpu.CompilerParams(
            collective_id=0, has_side_effects=True, vmem_limit_bytes=56 * 1024 * 1024
        ),
    )(*args)


def time_features(timestep):
    half = FREQ // 2
    freq_index = jnp.arange(half, dtype=F32)
    rates = jnp.exp(-math.log(10000.0) * freq_index / half)
    angles = timestep.astype(F32)[:, None] * rates[None, :]
    return jnp.concatenate([jnp.sin(angles), jnp.cos(angles)], axis=1).astype(BF16)


def local(
    context, stream, w_attn_out, modulation, w_teacher_head, noisy, timestep, frames,
    w_in, w_time, w_up, w_down, w_out,
):
    phase = (timestep.astype(F32) / STEPS + 0.008) / 1.008 * (math.pi / 2)
    frames_f = frames.astype(F32)
    info = jnp.stack([jnp.cos(phase)[0], jnp.sin(phase)[0], frames_f[0]])
    info = jnp.broadcast_to(jnp.pad(info, (0, 5))[:, None], (8, 128))
    mod = jnp.concatenate(
        [modulation[0], jnp.broadcast_to(frames_f[:, None], (1, 4096)), jnp.zeros((4, 4096), F32)], axis=0
    )
    features = jnp.broadcast_to(time_features(timestep), (256, FREQ))
    nf = jnp.concatenate([noisy, features], axis=1).reshape(8, 32, 256)
    wit = jnp.concatenate([w_in, w_time], axis=0)
    wit = wit.reshape(256, 16, 4, 32).transpose(0, 2, 1, 3).reshape(256, 2048)
    up = w_up.reshape(32, 16, 4, 6).transpose(1, 3, 2, 0).reshape(16, 6, 128)
    down = w_down.reshape(16, 4, 6, 32).transpose(0, 2, 1, 3).reshape(16, 6, 128)
    gap = jnp.zeros((16, 2, 128), BF16)
    pieces = jnp.concatenate([up, gap, down, gap], axis=1)
    target, grad, loss = call(
        context.reshape(8, 32, 512), w_attn_out.T, pieces, stream, mod, w_teacher_head, nf, info, w_out, wit
    )
    grad = grad[:, 0:6].reshape(16, 6, 4, 32).transpose(3, 0, 2, 1).reshape(32, 384)
    return target.reshape(256, C), loss[0, 0], grad


def solution(mesh):
    in_specs = (
        P("dp", "tp"),
        P("dp", None),
        P("tp", "dp"),
        P("dp", None, None),
        P("dp", None),
        P("dp", None),
        P("dp"),
        P("dp"),
        P(),
        P(),
        P("dp", "tp"),
        P("tp", "dp"),
        P("dp", None),
    )
    out_specs = (P("dp", None), P(), P("dp", "tp"))
    return jax.shard_map(local, mesh=mesh, in_specs=in_specs, out_specs=out_specs, check_vma=False)
```

time: 2210 us -> 191 us (0.09)
  the two profiles are of different devices: /device:TPU:128 before, /device:TPU:96 now
where the time goes in v1:
time: 191 us; the launch traced here: 190 us
  Pallas kernels  174 us (91%)
  local copies, waits for them, and re-layouts  11.1 us (6%)
  other arithmetic  3.23 us (2%)
  between operations  2.23 us (1%)
    pallas_call x1, Pallas kernels, call(): pl.pallas_call(body, out_shape=(jax.ShapeDtypeStruct((8, 32, 128), F32),...  174 us
    unnamed x11, local copies, waits for them, and re-layouts  6.01 us

profile of v1, /device:TPU:96, one launch (start us, length us, event | category | flops | bytes accessed | tf_op | source)
XLA Modules:
  0.0 190.4 jit_solution(10346451754344395984)
XLA Ops:
  2.1 0.1 select_maximum_fusion
  2.2 0.7 broadcast_in_dim.32.info
  2.9 0.1 pad_maximum_fusion.3
  3.0 1.5 pad_maximum_fusion.1
  4.5 0.1 pad.15.clone
  4.5 0.8 copy.39
  5.4 0.1 pad.16.clone
  5.5 0.7 maximum_maximum_fusion.mod
  6.2 1.3 copy.26
  7.5 1.3 copy.27
  8.8 0.1 pad_maximum_fusion
  9.0 0.0 copy-start
  9.0 0.0 copy-start.1
  9.0 0.1 copy.28
  9.1 1.4 copy.29.wit
  10.5 0.0 copy-done
  10.5 0.1 copy.20
  10.6 0.1 reshape.68
  10.7 0.1 reshape.78
  10.8 0.0 copy-done.1
  10.8 0.1 copy.22
  11.0 0.1 reshape.70
  11.1 0.1 reshape.79
  11.2 0.7 pad_maximum_fusion.2.sp
  11.9 173.9 %shard_map.148 = (f32[8,32,128]{2,1,0:T(8,128)}, f32[16,8,128]{2,1,0:T(8,128)}, f32[8,128]{1,0:T(8,128)}) custom-call(bf16[8,32,512]{2,1,0:T(8,128)(2,1)} %bitcast.30, bf16[64,512]{1,0:T(8,128)(2,1)} %bitcast.33, bf16[16,16,128]{2,1,0:T(8,128)(2,1)} %pad_maximum_fusion.2.sp, bf16[256,4096]{1,0:T(8,128)(2,1)} %stream.1, f32[8,4096]{1,0:T(8,128)} %maximum_maximum_fusion.mod, ...), custom_call_target="tpu_custom_call" | custom-call | tf_op jit(solution)/shard_map/pallas_call | solution.py:491
  185.8 0.9 copy.30
  186.7 0.1 reshape.76
  186.8 0.1 copy.31
  187.0 0.7 copy.32
  187.7 1.2 slice.6
  188.9 1.6 copy.43
  (6 shorter events, 0.2 us)
Async XLA Ops:
  9.0 1.5 copy-start
  9.0 1.9 copy-start.1

commit v2 on v1

--- a/solution.py
+++ b/solution.py
@@ -19,7 +19,7 @@
 
 COUNTS = dict(
     ctx=8, ag=128, ring=36, sib=32, sp=16, st=16, mod=16, head=4, nf=16, wo1=4, wo2=16, cnt=4,
-    dn=16, un=32, tm=16, gp=16, lx=16, tg=8, lt=8, lz=4, g1=4, g2=4, g3=4, g4=16,
+    dnx=4, dny=4, dn2x=4, dn2y=4, fr=16, un=32, tm=16, gp=16, lx=16, tg=8, lt=8, lz=4, g1=4, g2=4, g3=4, g4=16,
 )
 BASE = {}
 N_RECV = 0
@@ -49,11 +49,12 @@
 
 
 def body(
-    ctx, wt, sp, stream, mod, head, nf, info, wo, wit,
+    ctx, wa, wu, wd, stream, mod, head, noisy, info, wo, win, wtime,
     tgt_out, grad_out, loss_out,
-    ctxp, w4, s4, srecv, strb, modb, headb, nfb, woutb, lifted, slope, hidden, dnsend, dnrecv,
+    ctxp, w4, s4, sp, srecv, strb, modb, headb, nfb, woutb, wit, lifted, slope, hidden, dnsend,
+    dnx, dny, sx, sy, dn2x, dn2y,
     unitb, ubuf, gbuf, att, zbuf, tsend, trecv, gpb, tgb, g1, r1, g2, r2, g3, r3, g4s, g4r,
-    lx, lt, lz, cz, send_sem, recv_sem,
+    lx, lt, lz, fr, cz, send_sem, recv_sem,
 ):
     tp = lax.axis_index("tp")
     dp = lax.axis_index("dp")
@@ -182,26 +183,36 @@
     for d in (1, 2, 7, 6, 3, 5, 4):
         t = lax.rem(tp + d, 8)
         send(ctx.at[t], ctxp.at[tp, xy], "ctx", tp, t, dp)
+    selects = [select_units(q) for q in range(4)]
+    up = [dot_nt(selects[q], wu[...]) for q in range(4)]
+    down = [dot_nn(selects[q], wd[...]) for q in range(4)]
+    sp[:, 0:8] = jnp.concatenate(up, axis=1).reshape(16, 8, 128).astype(BF16)
+    sp[:, 8:16] = jnp.concatenate(down, axis=1).reshape(16, 8, 128).astype(BF16)
+    srecv[xy] = sp[xy]
     to_plane(lambda p: sp.at[p], srecv, "sp")
-    srecv[xy] = sp[xy]
-    w4[tp, zl] = wt[...]
+    nfb[xy, :, 0:128] = noisy[tp]
+    nfb[xy, :, 128:256] = jnp.broadcast_to(info[3:4], (32, 128)).astype(BF16)
+    to_plane(lambda p: nfb.at[xy], nfb, "nf")
+    w4[tp, zl] = wa[...].astype(F32).T.astype(BF16)
     ring_start(0)
-    nfb[xy] = nf[tp]
-    to_plane(lambda p: nf.at[tp], nfb, "nf")
     woutb[zl, xy] = wo[...]
     headb[zl] = head[...]
     for d in (1, 2, 3):
         other_dp = xy * 4 + other(zl, d)
         send(wo, woutb.at[zl, xy], "wo1", zl, tp, other_dp)
         send(head, headb.at[zl], "head", zl, tp, other_dp)
-    modb[xy] = mod[:, pl.ds(pl.multiple_of(xy * 256, 256), 256)]
-    to_plane(lambda p: mod.at[:, pl.ds(pl.multiple_of(p * 256, 256), 256)], modb, "mod")
     rows = pl.ds(pl.multiple_of(tp * 32, 32), 32)
     own_stream = pltpu.make_async_copy(
         stream.at[rows, pl.ds(pl.multiple_of(xy * 256, 256), 256)], strb.at[xy], send_sem.at[N_SEND - 1]
     )
     own_stream.start()
-    to_plane(lambda p: stream.at[rows, pl.ds(pl.multiple_of(p * 256, 256), 256)], strb, "st")
+
+    def small_sends():
+        modb[xy] = mod[0, :, pl.ds(pl.multiple_of(xy * 256, 256), 256)]
+        to_plane(lambda p: mod.at[0, :, pl.ds(pl.multiple_of(p * 256, 256), 256)], modb, "mod")
+        fr[xy] = jnp.broadcast_to(info[2:3], (8, 128))
+        to_plane(lambda p: fr.at[xy], fr, "fr")
+        to_plane(lambda p: stream.at[rows, pl.ds(pl.multiple_of(p * 256, 256), 256)], strb, "st")
 
     def ctx_own(chunk_step):
         chunk = other(zh, chunk_step)
@@ -240,46 +251,62 @@
             v = v / (1.0 + jnp.exp(-v))
             lifted[128 * block : 128 * block + 128, 512 * n : 512 * n + 512] = v.astype(BF16)
 
+    def rings(hop):
+        ring_step(1, hop)
+        ring_step(0, hop)
+
+    group128 = lax.div(lax.broadcasted_iota(jnp.int32, (128, 128), 1), 32)
+
+    def order_features(zo):
+        for half, source in ((0, win), (1, wtime)):
+            for t in range(4):
+                tile = jnp.zeros((128, 128), F32)
+                for g in range(4):
+                    piece = source[:, 128 * (4 * t + g) : 128 * (4 * t + g) + 128].astype(F32)
+                    shift = ((g - zo) * 32) % 128
+                    moved = pltpu.roll(piece, shift, 1) if shift else piece
+                    tile = jnp.where(group128 == g, moved, tile)
+                at = 512 * zo + 128 * t
+                wit[128 * half : 128 * half + 128, at : at + 128] = tile.astype(BF16)
+
+    order_features(0)
+    order_features(1)
+    rings(1)
+    order_features(2)
+    ctx_own(1)
+    order_features(3)
+    rings(2)
     from_plane(nfb, "nf")
-    ring_step(0, 1)
-    ring_step(1, 1)
+    ctx_own(3)
+    small_sends()
     lift(0)
-    ctx_own(1)
     ctx_forward(0)
-    ring_step(0, 2)
-    ring_step(1, 2)
+    rings(3)
+    ctx_own(2)
     lift(1)
-    ctx_own(3)
     ctx_forward(1)
+    rings(4)
     for d in (1, 2, 3):
         zo = other(zl, d)
         arrived(woutb.at[zo, xy], "wo1", zo)
     for dx, dy in XY:
         p = plane(dx, dy)
         send(woutb.at[:, xy], woutb.at[:, xy], "wo2", xy, tp, p * 4 + zl)
-    ring_step(0, 3)
-    ring_step(1, 3)
     lift(2)
-    ctx_own(2)
+    rings(5)
     ctx_forward(3)
-    ring_step(0, 4)
-    ring_step(1, 4)
     lift(3)
-    ring_step(0, 5)
-    ring_step(1, 5)
+    rings(6)
+    from_plane(fr, "fr")
+    count_part = fr[0]
+    for s in range(1, 16):
+        count_part = count_part + fr[s]
+    cz[zl] = count_part
+    for d in (1, 2, 3):
+        send(cz.at[zl], cz.at[zl], "cnt", zl, tp, xy * 4 + other(zl, d))
+    rings(7)
     ctx_forward(2)
-    ring_step(0, 6)
-    ring_step(1, 6)
-    from_plane(modb, "mod")
-    count_part = modb[0, 3:4, 0:128]
-    for s in range(1, 16):
-        count_part = count_part + modb[s, 3:4, 0:128]
-    cz[zl] = jnp.broadcast_to(count_part, (8, 128))
-    for d in (1, 2, 3):
-        send(cz.at[zl], cz.at[zl], "cnt", zl, tp, xy * 4 + other(zl, d))
-    for hop in (7, 8):
-        ring_step(0, hop)
-        ring_step(1, hop)
+    rings(8)
     ring_last(1)
 
     def up_part(zb):
@@ -301,15 +328,20 @@
         act = (0.5 * pre * (1.0 + tangent)).astype(BF16)
         for zb in range(4):
             part = dot_nn(act, down_part(zb)).astype(BF16)
-            dnsend[8 * block : 8 * block + 8, :, 512 * zb : 512 * zb + 512] = part.reshape(8, 32, 512)
-    dnrecv[xy] = dnsend[xy]
-    to_plane(lambda p: dnsend.at[p], dnrecv, "dn")
+            dnsend[2 * block : 2 * block + 2, :, :, 512 * zb : 512 * zb + 512] = part.reshape(2, 4, 32, 512)
+    dnx[x] = dnsend[x, :, :, 0:1024]
+    dny[y] = dnsend[:, y, :, 1024:2048]
+    for d in (1, 3, 2):
+        xo, yo = other(x, d), other(y, d)
+        send(dnsend.at[xo, :, :, pl.ds(0, 1024)], dnx.at[x], "dnx", x, tp, (xo * 4 + y) * 4 + zl)
+        send(dnsend.at[:, yo, :, pl.ds(1024, 1024)], dny.at[y], "dny", y, tp, (x * 4 + yo) * 4 + zl)
 
     ring_last(0)
     for d in (1, 2, 3):
         zo = other(zl, d)
         arrived(headb.at[zo], "head", zo)
     from_plane(strb, "st")
+    from_plane(modb, "mod")
     own_stream.wait()
     for step in (0, 1, 3, 2):
         gather_last(ctx_view(other(zh, step)), "ag", other(zh, step) * 32)
@@ -334,32 +366,47 @@
     lax.fori_loop(0, 16, norm_step, 0)
     whole_head = headb[...].reshape(256, 128)
     tsend[:, 0:32] = dot_nn(zbuf[...].reshape(512, 256), whole_head).reshape(16, 32, 128)
-    ones_row = (lax.broadcasted_iota(jnp.int32, (1, 8, 1), 1) == 2).astype(F32)
-    vectors = (modb[...] + ones_row).reshape(128, 256)
-    tsend[:, 64:72] = split_dot(vectors, whole_head).reshape(16, 8, 128)
+    vectors = jnp.concatenate([modb[:, 1], 1.0 + modb[:, 2]], axis=0)
+    vectors = split_dot(vectors, whole_head)
+    tsend[:, 65] = vectors[0:16]
+    tsend[:, 66] = vectors[16:32]
     trecv[xy] = tsend[xy]
     to_plane(lambda p: tsend.at[p], trecv, "tm")
 
-    from_plane(dnrecv, "dn")
+    for d in (1, 3, 2):
+        xo, yo = other(x, d), other(y, d)
+        arrived(dnx.at[xo], "dnx", xo)
+        arrived(dny.at[yo], "dny", yo)
+    for k in range(4):
+        sx[k] = sum(dnx[o, k].astype(F32) for o in range(4)).astype(BF16)
+        sy[k] = sum(dny[o, k].astype(F32) for o in range(4)).astype(BF16)
+    dn2x[y] = sx[y]
+    dn2y[x] = sy[x]
+    for d in (1, 3, 2):
+        xo, yo = other(x, d), other(y, d)
+        send(sx.at[yo], dn2x.at[y], "dn2x", y, tp, (x * 4 + yo) * 4 + zl)
+        send(sy.at[xo], dn2y.at[x], "dn2y", x, tp, (xo * 4 + y) * 4 + zl)
     from_plane(_Columns(woutb), "wo2")
-    own_nf = nf[tp]
-
-    def down_sum(s, total):
-        return total + dnrecv[s].astype(F32)
-
+    whole_out = woutb[...].reshape(2048, 128)
+    fold = dot_nn(down_part(0), whole_out[0:512])
+    for zb in range(1, 4):
+        fold = fold + dot_nn(down_part(zb), whole_out[512 * zb : 512 * zb + 512])
+    gbuf[...] = fold.astype(BF16)
+    own_nf = nfb[xy]
     mixed = dot_nn(own_nf, wit[...])
-    mixed = lax.fori_loop(0, 16, down_sum, mixed)
+    for d in (1, 3, 2):
+        xo, yo = other(x, d), other(y, d)
+        arrived(dn2x.at[yo], "dn2x", yo)
+        arrived(dn2y.at[xo], "dn2y", xo)
+    down_x = sum(dn2x[o].astype(F32) for o in range(4))
+    down_y = sum(dn2y[o].astype(F32) for o in range(4))
+    mixed = mixed + jnp.concatenate([down_x, down_y], axis=1)
     inv_rms = lax.rsqrt(jnp.mean(mixed * mixed, axis=-1, keepdims=True) + EPS)
     unit_b = (mixed * inv_rms).astype(BF16)
     unitb[xy] = unit_b
     gather_own(unit_view, "un", 0)
-    whole_out = woutb[...].reshape(2048, 128)
     pred = dot_nn(unit_b, whole_out)
     gather_forward(unit_view, "un", 0)
-    fold = dot_nn(down_part(0), whole_out[0:512])
-    for zb in range(1, 4):
-        fold = fold + dot_nn(down_part(zb), whole_out[512 * zb : 512 * zb + 512])
-    gbuf[...] = fold.astype(BF16)
 
     for d in (1, 2, 3):
         zo = other(zl, d)
@@ -466,10 +513,27 @@
         arrived(tgb.at[t], "tg", t)
     tgt_out[...] = tgb[...]
     from_plane(g4r, "g4")
-    grad_out[...] = g4r[...]
+    part = g4r[...].reshape(128, 128)
+    high = part.astype(BF16)
+    part = part - high.astype(F32)
+    middle = part.astype(BF16)
+    low = (part - middle.astype(F32)).astype(BF16)
+    grad = jnp.zeros((32, 384), F32)
+    for q in range(4):
+        chosen = dot_tn(high, selects[q]) + dot_tn(middle, selects[q]) + dot_tn(low, selects[q])
+        grad = grad + chosen[32 * q : 32 * q + 32]
+    grad_out[...] = grad
     for copy in sends:
         copy.wait_send()
     assert len(sends) < N_SEND
+
+
+def select_units(q):
+    row = lax.broadcasted_iota(jnp.int32, (128, 384), 0)
+    unit = lax.broadcasted_iota(jnp.int32, (128, 384), 1)
+    r = lax.rem(row, 8)
+    chosen = (unit == lax.div(row, 8) * 24 + q * 6 + r) & (r < 6)
+    return jnp.where(chosen, 1.0, 0.0).astype(BF16)
 
 
 class _Columns:
@@ -492,26 +556,33 @@
         body,
         out_shape=(
             jax.ShapeDtypeStruct((8, 32, 128), F32),
-            jax.ShapeDtypeStruct((16, 8, 128), F32),
+            jax.ShapeDtypeStruct((32, 384), F32),
             jax.ShapeDtypeStruct((8, 128), F32),
         ),
-        in_specs=[vmem, vmem, vmem, hbm, vmem, vmem, vmem, vmem, vmem, vmem],
+        in_specs=[vmem] * 4 + [hbm] + [vmem] * 7,
         out_specs=(vmem, vmem, vmem),
         scratch_shapes=[
             V((8, 16, 32, 512), BF16),
             V((8, 4, 64, 512), BF16),
             V((2, 4, 4, 64, 512), BF16),
             V((16, 16, 128), BF16),
+            V((16, 16, 128), BF16),
             V((16, 32, 256), BF16),
-            V((16, 8, 256), F32),
+            V((16, 3, 256), F32),
             V((4, 64, 128), BF16),
             V((16, 32, 256), BF16),
             V((4, 16, 32, 128), BF16),
+            V((256, 2048), BF16),
             V((512, 2048), BF16),
             V((512, 256), F32),
             V((64, 512), F32),
-            V((16, 32, 2048), BF16),
-            V((16, 32, 2048), BF16),
+            V((4, 4, 32, 2048), BF16),
+            V((4, 4, 32, 1024), BF16),
+            V((4, 4, 32, 1024), BF16),
+            V((4, 32, 1024), BF16),
+            V((4, 32, 1024), BF16),
+            V((4, 32, 1024), BF16),
+            V((4, 32, 1024), BF16),
             V((16, 32, 2048), BF16),
             V((512, 256), F32),
             V((256, 128), BF16),
@@ -532,6 +603,7 @@
             V((16, 8, 128), F32),
             V((8, 8, 128), F32),
             V((4, 8, 128), F32),
+            V((16, 8, 128), F32),
             V((4, 8, 128), F32),
             pltpu.SemaphoreType.DMA((N_SEND,)),
             pltpu.SemaphoreType.DMA((N_RECV,)),
@@ -555,24 +627,15 @@
     w_in, w_time, w_up, w_down, w_out,
 ):
     phase = (timestep.astype(F32) / STEPS + 0.008) / 1.008 * (math.pi / 2)
-    frames_f = frames.astype(F32)
-    info = jnp.stack([jnp.cos(phase)[0], jnp.sin(phase)[0], frames_f[0]])
-    info = jnp.broadcast_to(jnp.pad(info, (0, 5))[:, None], (8, 128))
-    mod = jnp.concatenate(
-        [modulation[0], jnp.broadcast_to(frames_f[:, None], (1, 4096)), jnp.zeros((4, 4096), F32)], axis=0
+    scalars = jnp.stack([jnp.cos(phase)[0], jnp.sin(phase)[0], frames.astype(F32)[0]])
+    features = time_features(timestep).astype(F32)
+    info = jnp.concatenate(
+        [jnp.broadcast_to(scalars[:, None], (3, 128)), features, jnp.zeros((4, 128), F32)], axis=0
     )
-    features = jnp.broadcast_to(time_features(timestep), (256, FREQ))
-    nf = jnp.concatenate([noisy, features], axis=1).reshape(8, 32, 256)
-    wit = jnp.concatenate([w_in, w_time], axis=0)
-    wit = wit.reshape(256, 16, 4, 32).transpose(0, 2, 1, 3).reshape(256, 2048)
-    up = w_up.reshape(32, 16, 4, 6).transpose(1, 3, 2, 0).reshape(16, 6, 128)
-    down = w_down.reshape(16, 4, 6, 32).transpose(0, 2, 1, 3).reshape(16, 6, 128)
-    gap = jnp.zeros((16, 2, 128), BF16)
-    pieces = jnp.concatenate([up, gap, down, gap], axis=1)
     target, grad, loss = call(
-        context.reshape(8, 32, 512), w_attn_out.T, pieces, stream, mod, w_teacher_head, nf, info, w_out, wit
+        context.reshape(8, 32, 512), w_attn_out, w_up, w_down, stream, modulation, w_teacher_head,
+        noisy.reshape(8, 32, 128), info, w_out, w_in, w_time,
     )
-    grad = grad[:, 0:6].reshape(16, 6, 4, 32).transpose(3, 0, 2, 1).reshape(32, 384)
     return target.reshape(256, C), loss[0, 0], grad
 
 

time: 191 us -> 170 us (0.89)
  Pallas kernels: 174 us -> 158 us
  other arithmetic: 3.23 us -> 0.87 us
  local copies, waits for them, and re-layouts: 11.1 us -> 8.78 us
    pallas_call x1, Pallas kernels: 174 us -> 158 us  [call(): pl.pallas_call(body, out_shape=(jax.ShapeDtypeStruct((8, 32, 128), F32),...]
    concatenate x4 -> x1, other arithmetic: 3.03 us -> 0.67 us  [local(): jnp.concatenate([jnp.broadcast_to(scalars[:, None], (3, 128)), features,...]
    reshape x9 -> x0, local copies, waits for them, and re-layouts: 1.98 us -> none  [the longest x1 1.41 us: local(): wit = wit.reshape(256, 16, 4, 32).transpose(0, 2, 1, 3).reshape(256, 2048)]
    unnamed x11 -> x5, local copies, waits for them, and re-layouts: 6.01 us -> 7.51 us
where the time goes in v2:
time: 170 us
  Pallas kernels  158 us (93%)
  local copies, waits for them, and re-layouts  8.78 us (5%)
  between operations  2.1 us (1%)
    pallas_call x1, Pallas kernels, call(): pl.pallas_call(body, out_shape=(jax.ShapeDtypeStruct((8, 32, 128), F32),...  158 us
    unnamed x5, local copies, waits for them, and re-layouts  7.51 us

profile of v2, /device:TPU:96, one launch (start us, length us, event | category | flops | bytes accessed | tf_op | source)
XLA Modules:
  0.0 169.8 jit_solution(5362168327943020774)
XLA Ops:
  2.1 0.1 pad_maximum_fusion
  2.2 0.1 pad.2.clone
  2.3 0.1 maximum_convert_fusion
  2.4 0.7 maximum_maximum_fusion.info
  3.0 1.4 copy.18.mod
  4.5 1.5 copy.17.wd
  6.0 1.6 copy.16.wa
  7.6 158.0 %shard_map.148 = (f32[8,32,128]{2,1,0:T(8,128)}, f32[32,384]{1,0:T(8,128)}, f32[8,128]{1,0:T(8,128)}) custom-call(bf16[8,32,512]{2,1,0:T(8,128)(2,1)} %bitcast.9, bf16[512,64]{1,0:T(8,128)(2,1)} %copy.16.wa, bf16[32,384]{1,0:T(8,128)(2,1)} %wu.1, bf16[384,32]{1,0:T(8,128)(2,1)} %copy.17.wd, bf16[256,4096]{1,0:T(8,128)(2,1)} %stream.1, ...), custom_call_target="tpu_custom_call" | custom-call | tf_op jit(solution)/shard_map/pallas_call | solution.py:555
  165.6 1.2 slice.3
  166.8 1.6 copy.23
  168.4 1.4 copy.24
  (2 shorter events, 0.1 us)

commit v3 on v2

--- a/solution.py
+++ b/solution.py
@@ -19,7 +19,7 @@
 
 COUNTS = dict(
     ctx=8, ag=128, ring=36, sib=32, sp=16, st=16, mod=16, head=4, nf=16, wo1=4, wo2=16, cnt=4,
-    dnx=4, dny=4, dn2x=4, dn2y=4, fr=16, un=32, tm=16, gp=16, lx=16, tg=8, lt=8, lz=4, g1=4, g2=4, g3=4, g4=16,
+    dnx=4, dny=4, dn2x=4, dn2y=4, un=32, tm=16, gp=16, lx=16, tg=8, lt=8, lz=4, g1=4, g2=4, g3=4, g4=16,
 )
 BASE = {}
 N_RECV = 0
@@ -54,7 +54,7 @@
     ctxp, w4, s4, sp, srecv, strb, modb, headb, nfb, woutb, wit, lifted, slope, hidden, dnsend,
     dnx, dny, sx, sy, dn2x, dn2y,
     unitb, ubuf, gbuf, att, zbuf, tsend, trecv, gpb, tgb, g1, r1, g2, r2, g3, r3, g4s, g4r,
-    lx, lt, lz, fr, cz, send_sem, recv_sem,
+    lx, lt, lz, cz, send_sem, recv_sem,
 ):
     tp = lax.axis_index("tp")
     dp = lax.axis_index("dp")
@@ -185,15 +185,17 @@
         send(ctx.at[t], ctxp.at[tp, xy], "ctx", tp, t, dp)
     selects = [select_units(q) for q in range(4)]
     up = [dot_nt(selects[q], wu[...]) for q in range(4)]
-    down = [dot_nn(selects[q], wd[...]) for q in range(4)]
+    down = [dot_nt(selects[q], wd[...]) for q in range(4)]
     sp[:, 0:8] = jnp.concatenate(up, axis=1).reshape(16, 8, 128).astype(BF16)
     sp[:, 8:16] = jnp.concatenate(down, axis=1).reshape(16, 8, 128).astype(BF16)
     srecv[xy] = sp[xy]
     to_plane(lambda p: sp.at[p], srecv, "sp")
-    nfb[xy, :, 0:128] = noisy[tp]
-    nfb[xy, :, 128:256] = jnp.broadcast_to(info[3:4], (32, 128)).astype(BF16)
+    nfb[xy, 0:32, 0:128] = noisy[tp]
+    nfb[xy, 0:32, 128:256] = jnp.broadcast_to(info[3:4], (32, 128)).astype(BF16)
+    nfb[xy, 32:48, 0:128] = jnp.broadcast_to(info[2:3], (16, 128)).astype(BF16)
+    nfb[xy, 32:48, 128:256] = jnp.zeros((16, 128), BF16)
     to_plane(lambda p: nfb.at[xy], nfb, "nf")
-    w4[tp, zl] = wa[...].astype(F32).T.astype(BF16)
+    w4[tp, zl] = wa[...]
     ring_start(0)
     woutb[zl, xy] = wo[...]
     headb[zl] = head[...]
@@ -208,10 +210,8 @@
     own_stream.start()
 
     def small_sends():
-        modb[xy] = mod[0, :, pl.ds(pl.multiple_of(xy * 256, 256), 256)]
-        to_plane(lambda p: mod.at[0, :, pl.ds(pl.multiple_of(p * 256, 256), 256)], modb, "mod")
-        fr[xy] = jnp.broadcast_to(info[2:3], (8, 128))
-        to_plane(lambda p: fr.at[xy], fr, "fr")
+        modb[xy] = mod[:, :, pl.ds(pl.multiple_of(xy * 256, 256), 256)]
+        to_plane(lambda p: mod.at[:, :, pl.ds(pl.multiple_of(p * 256, 256), 256)], modb, "mod")
         to_plane(lambda p: stream.at[rows, pl.ds(pl.multiple_of(p * 256, 256), 256)], strb, "st")
 
     def ctx_own(chunk_step):
@@ -245,15 +245,11 @@
     ctx_own(0)
 
     def lift(block):
-        piece = nfb[4 * block : 4 * block + 4].reshape(128, 256)
+        piece = nfb[4 * block : 4 * block + 4, 0:32].reshape(128, 256)
         for n in range(4):
             v = dot_nn(piece, wit[:, 512 * n : 512 * n + 512])
             v = v / (1.0 + jnp.exp(-v))
             lifted[128 * block : 128 * block + 128, 512 * n : 512 * n + 512] = v.astype(BF16)
-
-    def rings(hop):
-        ring_step(1, hop)
-        ring_step(0, hop)
 
     group128 = lax.div(lax.broadcasted_iota(jnp.int32, (128, 128), 1), 32)
 
@@ -269,45 +265,7 @@
                 at = 512 * zo + 128 * t
                 wit[128 * half : 128 * half + 128, at : at + 128] = tile.astype(BF16)
 
-    order_features(0)
-    order_features(1)
-    rings(1)
-    order_features(2)
-    ctx_own(1)
-    order_features(3)
-    rings(2)
-    from_plane(nfb, "nf")
-    ctx_own(3)
-    small_sends()
-    lift(0)
-    ctx_forward(0)
-    rings(3)
-    ctx_own(2)
-    lift(1)
-    ctx_forward(1)
-    rings(4)
-    for d in (1, 2, 3):
-        zo = other(zl, d)
-        arrived(woutb.at[zo, xy], "wo1", zo)
-    for dx, dy in XY:
-        p = plane(dx, dy)
-        send(woutb.at[:, xy], woutb.at[:, xy], "wo2", xy, tp, p * 4 + zl)
-    lift(2)
-    rings(5)
-    ctx_forward(3)
-    lift(3)
-    rings(6)
-    from_plane(fr, "fr")
-    count_part = fr[0]
-    for s in range(1, 16):
-        count_part = count_part + fr[s]
-    cz[zl] = count_part
-    for d in (1, 2, 3):
-        send(cz.at[zl], cz.at[zl], "cnt", zl, tp, xy * 4 + other(zl, d))
-    rings(7)
-    ctx_forward(2)
-    rings(8)
-    ring_last(1)
+    k0 = math.sqrt(2.0 / math.pi)
 
     def up_part(zb):
         return s4[:, :, zb, 0:32, :].reshape(256, 512)
@@ -315,8 +273,7 @@
     def down_part(zb):
         return s4[:, :, zb, 32:64, :].reshape(256, 512)
 
-    k0 = math.sqrt(2.0 / math.pi)
-    for block in range(2):
+    def student(block):
         rs = slice(256 * block, 256 * block + 256)
         pre = dot_nt(lifted[rs, 0:512], up_part(0))
         for zb in range(1, 4):
@@ -329,50 +286,68 @@
         for zb in range(4):
             part = dot_nn(act, down_part(zb)).astype(BF16)
             dnsend[2 * block : 2 * block + 2, :, :, 512 * zb : 512 * zb + 512] = part.reshape(2, 4, 32, 512)
-    dnx[x] = dnsend[x, :, :, 0:1024]
-    dny[y] = dnsend[:, y, :, 1024:2048]
+
+    def share_out():
+        for d in (1, 2, 3):
+            zo = other(zl, d)
+            arrived(woutb.at[zo, xy], "wo1", zo)
+        for dx, dy in XY:
+            p = plane(dx, dy)
+            send(woutb.at[:, xy], woutb.at[:, xy], "wo2", xy, tp, p * 4 + zl)
+
+    def share_count():
+        count_part = nfb[0, 32:40, 0:128].astype(F32)
+        for s in range(1, 16):
+            count_part = count_part + nfb[s, 32:40, 0:128].astype(F32)
+        cz[zl] = count_part
+        for d in (1, 2, 3):
+            send(cz.at[zl], cz.at[zl], "cnt", zl, tp, xy * 4 + other(zl, d))
+
+    small_sends()
+    order_features(0)
+    ring_step(1, 1)
+    ring_step(0, 1)
+    ctx_own(1)
+    order_features(1)
+    ring_step(1, 2)
+    ring_step(0, 2)
+    ctx_own(3)
+    order_features(2)
+    order_features(3)
+    ring_step(1, 3)
+    ring_step(0, 3)
+    share_out()
+    ctx_own(2)
+    from_plane(nfb, "nf")
+    ctx_forward(0)
+    ring_step(1, 4)
+    ring_step(0, 4)
+    lift(0)
+    lift(1)
+    ctx_forward(1)
+    ring_step(1, 5)
+    ring_step(0, 5)
+    lift(2)
+    lift(3)
+    ring_step(1, 6)
+    ring_step(0, 6)
+    ctx_forward(3)
+    share_count()
+    ring_step(1, 7)
+    ring_step(0, 7)
+    ctx_forward(2)
+    ring_step(1, 8)
+    ring_step(0, 8)
+    ring_last(1)
+    student(0)
+    student(1)
     for d in (1, 3, 2):
         xo, yo = other(x, d), other(y, d)
         send(dnsend.at[xo, :, :, pl.ds(0, 1024)], dnx.at[x], "dnx", x, tp, (xo * 4 + y) * 4 + zl)
         send(dnsend.at[:, yo, :, pl.ds(1024, 1024)], dny.at[y], "dny", y, tp, (x * 4 + yo) * 4 + zl)
-
+    dnx[x] = dnsend[x, :, :, 0:1024]
+    dny[y] = dnsend[:, y, :, 1024:2048]
     ring_last(0)
-    for d in (1, 2, 3):
-        zo = other(zl, d)
-        arrived(headb.at[zo], "head", zo)
-    from_plane(strb, "st")
-    from_plane(modb, "mod")
-    own_stream.wait()
-    for step in (0, 1, 3, 2):
-        gather_last(ctx_view(other(zh, step)), "ag", other(zh, step) * 32)
-    att[...] = jnp.zeros_like(att)
-
-    def att_step(t, carry):
-        att[...] += dot_nt(ctxp[t].reshape(512, 512), w4[t].reshape(256, 512))
-        return carry
-
-    lax.fori_loop(0, 8, att_step, 0)
-    lane = lax.broadcasted_iota(jnp.int32, (32, 128), 1)
-
-    def norm_step(s, carry):
-        state = strb[s].astype(F32) + modb[s, 0:1] * att[pl.ds(pl.multiple_of(s * 32, 32), 32)]
-        center = jnp.mean(state, axis=-1, keepdims=True)
-        state = state - center
-        square = jnp.sum(state * state, axis=-1, keepdims=True)
-        zbuf[s] = (state * (1.0 + modb[s, 2:3])).astype(BF16)
-        tsend[s, 32:64] = jnp.where(lane < 64, center, square)
-        return carry
-
-    lax.fori_loop(0, 16, norm_step, 0)
-    whole_head = headb[...].reshape(256, 128)
-    tsend[:, 0:32] = dot_nn(zbuf[...].reshape(512, 256), whole_head).reshape(16, 32, 128)
-    vectors = jnp.concatenate([modb[:, 1], 1.0 + modb[:, 2]], axis=0)
-    vectors = split_dot(vectors, whole_head)
-    tsend[:, 65] = vectors[0:16]
-    tsend[:, 66] = vectors[16:32]
-    trecv[xy] = tsend[xy]
-    to_plane(lambda p: tsend.at[p], trecv, "tm")
-
     for d in (1, 3, 2):
         xo, yo = other(x, d), other(y, d)
         arrived(dnx.at[xo], "dnx", xo)
@@ -386,13 +361,27 @@
         xo, yo = other(x, d), other(y, d)
         send(sx.at[yo], dn2x.at[y], "dn2x", y, tp, (x * 4 + yo) * 4 + zl)
         send(sy.at[xo], dn2y.at[x], "dn2y", x, tp, (xo * 4 + y) * 4 + zl)
+
+    for d in (1, 2, 3):
+        zo = other(zl, d)
+        arrived(headb.at[zo], "head", zo)
+    for step in (0, 1, 3, 2):
+        gather_last(ctx_view(other(zh, step)), "ag", other(zh, step) * 32)
+    att[...] = jnp.zeros_like(att)
+
+    def att_step(t, carry):
+        att[...] += dot_nt(ctxp[t].reshape(512, 512), w4[t].reshape(256, 512))
+        return carry
+
+    lax.fori_loop(0, 8, att_step, 0)
+
     from_plane(_Columns(woutb), "wo2")
     whole_out = woutb[...].reshape(2048, 128)
     fold = dot_nn(down_part(0), whole_out[0:512])
     for zb in range(1, 4):
         fold = fold + dot_nn(down_part(zb), whole_out[512 * zb : 512 * zb + 512])
     gbuf[...] = fold.astype(BF16)
-    own_nf = nfb[xy]
+    own_nf = nfb[xy, 0:32]
     mixed = dot_nn(own_nf, wit[...])
     for d in (1, 3, 2):
         xo, yo = other(x, d), other(y, d)
@@ -406,7 +395,32 @@
     unitb[xy] = unit_b
     gather_own(unit_view, "un", 0)
     pred = dot_nn(unit_b, whole_out)
+
+    from_plane(strb, "st")
+    from_plane(modb, "mod")
+    own_stream.wait()
+    lane = lax.broadcasted_iota(jnp.int32, (32, 128), 1)
+
+    def norm_step(s, carry):
+        state = strb[s].astype(F32) + modb[s, 0] * att[pl.ds(pl.multiple_of(s * 32, 32), 32)]
+        center = jnp.mean(state, axis=-1, keepdims=True)
+        state = state - center
+        square = jnp.sum(state * state, axis=-1, keepdims=True)
+        zbuf[s] = (state * (1.0 + modb[s, 2])).astype(BF16)
+        tsend[s, 32:64] = jnp.where(lane < 64, center, square)
+        return carry
+
+    lax.fori_loop(0, 16, norm_step, 0)
+    whole_head = headb[...].reshape(256, 128)
+    tsend[:, 0:32] = dot_nn(zbuf[...].reshape(512, 256), whole_head).reshape(16, 32, 128)
+    vectors = jnp.concatenate([modb[:, 1, 0], 1.0 + modb[:, 2, 0]], axis=0)
+    vectors = split_dot(vectors, whole_head)
+    tsend[:, 65] = vectors[0:16]
+    tsend[:, 66] = vectors[16:32]
+    trecv[xy] = tsend[xy]
+    to_plane(lambda p: tsend.at[p], trecv, "tm")
     gather_forward(unit_view, "un", 0)
+
 
     for d in (1, 2, 3):
         zo = other(zl, d)
@@ -454,16 +468,24 @@
     both = gpb[...].reshape(512, 256)
     grad_hidden = dot_nt(both[:, 0:128], gbuf[...]) - both[:, 128:129].astype(F32) * ubuf[...]
     grad_pre = (grad_hidden * slope[...]).astype(BF16)
-    for zb in range(4):
-        g1[:, :, zb] = dot_tn(grad_pre, lifted[:, 512 * zb : 512 * zb + 512]).reshape(2, 4, 32, 512)
-        send(g1.at[1 - c, :, zb], r1.at[:, zb], "g1", zb, sibling, dp)
-    for zb in range(4):
-        arrived(r1.at[:, zb], "g1", zb)
-        g2[zb] = (g1[c, :, zb] + r1[:, zb]).astype(BF16)
+
+    def both_cores(zb):
+        arrived(r1.at[zb], "g1", zb)
+        g2[zb] = (g1[zb, c] + r1[zb]).astype(BF16)
+        if zb is not zl:
+            send(g2.at[zb], r2.at[zl], "g2", zl, tp, xy * 4 + zb)
+
+    previous = None
+    for d in (2, 1, 3, 0):
+        zb = other(zl, d) if d else zl
+        columns = pl.ds(pl.multiple_of(zb * 512, 512), 512)
+        g1[zb] = dot_tn(grad_pre, lifted[:, columns]).reshape(2, 4, 32, 512)
+        send(g1.at[zb, 1 - c], r1.at[zb], "g1", zb, sibling, dp)
+        if previous is not None:
+            both_cores(previous)
+        previous = zb
+    both_cores(zl)
     r2[zl] = g2[zl]
-    for d in (1, 2, 3):
-        zo = other(zl, d)
-        send(g2.at[zo], r2.at[zl], "g2", zl, tp, xy * 4 + zo)
     from_plane(lx, "lx")
     loss_sum = lx[0]
     for s in range(1, 16):
@@ -568,9 +590,9 @@
             V((16, 16, 128), BF16),
             V((16, 16, 128), BF16),
             V((16, 32, 256), BF16),
-            V((16, 3, 256), F32),
+            V((16, 3, 1, 256), F32),
             V((4, 64, 128), BF16),
-            V((16, 32, 256), BF16),
+            V((16, 48, 256), BF16),
             V((4, 16, 32, 128), BF16),
             V((256, 2048), BF16),
             V((512, 2048), BF16),
@@ -592,7 +614,7 @@
             V((16, 72, 128), F32),
             V((16, 32, 256), BF16),
             V((8, 32, 128), F32),
-            V((2, 4, 4, 32, 512), F32),
+            V((4, 2, 4, 32, 512), F32),
             V((4, 4, 32, 512), F32),
             V((4, 4, 32, 512), BF16),
             V((4, 4, 32, 512), BF16),
@@ -603,7 +625,6 @@
             V((16, 8, 128), F32),
             V((8, 8, 128), F32),
             V((4, 8, 128), F32),
-            V((16, 8, 128), F32),
             V((4, 8, 128), F32),
             pltpu.SemaphoreType.DMA((N_SEND,)),
             pltpu.SemaphoreType.DMA((N_RECV,)),
@@ -633,7 +654,7 @@
         [jnp.broadcast_to(scalars[:, None], (3, 128)), features, jnp.zeros((4, 128), F32)], axis=0
     )
     target, grad, loss = call(
-        context.reshape(8, 32, 512), w_attn_out, w_up, w_down, stream, modulation, w_teacher_head,
+        context.reshape(8, 32, 512), w_attn_out.T, w_up, w_down.T, stream, modulation.reshape(3, 1, 4096), w_teacher_head,
         noisy.reshape(8, 32, 128), info, w_out, w_in, w_time,
     )
     return target.reshape(256, C), loss[0, 0], grad

time: 170 us -> 160 us (0.941)
  the two profiles are of different devices: /device:TPU:96 before, /device:TPU:32 now
where the time goes in v3:
time: 160 us
  Pallas kernels  152 us (95%)
  local copies, waits for them, and re-layouts  4.25 us (3%)
  between operations  2.1 us (1%)
    pallas_call x1, Pallas kernels, call(): pl.pallas_call(body, out_shape=(jax.ShapeDtypeStruct((8, 32, 128), F32),...  152 us

profile of v3, /device:TPU:32, one launch (start us, length us, event | category | flops | bytes accessed | tf_op | source)
XLA Modules:
  0.0 159.5 jit_solution(14751339302493742572)
XLA Ops:
  2.1 0.1 pad_maximum_fusion
  2.2 0.1 pad.2.clone
  2.3 0.1 maximum_convert_fusion
  2.4 0.7 maximum_maximum_fusion.info
  3.0 152.3 %shard_map.148 = (f32[8,32,128]{2,1,0:T(8,128)}, f32[32,384]{1,0:T(8,128)}, f32[8,128]{1,0:T(8,128)}) custom-call(bf16[8,32,512]{2,1,0:T(8,128)(2,1)} %bitcast.12, bf16[64,512]{1,0:T(8,128)(2,1)} %bitcast.14, bf16[32,384]{1,0:T(8,128)(2,1)} %wu.1, bf16[32,384]{1,0:T(8,128)(2,1)} %bitcast.17, bf16[256,4096]{1,0:T(8,128)(2,1)} %stream.1, ...), custom_call_target="tpu_custom_call" | custom-call | tf_op jit(solution)/shard_map/pallas_call | solution.py:577
  155.3 1.2 slice.3
  156.5 1.6 copy.20
  158.1 1.4 copy.21
  (2 shorter events, 0.1 us)

commit v4 on v3

--- a/solution.py
+++ b/solution.py
@@ -51,7 +51,7 @@
 def body(
     ctx, wa, wu, wd, stream, mod, head, noisy, info, wo, win, wtime,
     tgt_out, grad_out, loss_out,
-    ctxp, w4, s4, sp, srecv, strb, modb, headb, nfb, woutb, wit, lifted, slope, hidden, dnsend,
+    ctxp, w4, s4, upw, dnw, sp, srecv, strb, modb, headb, nfb, woutb, wit, lifted, slope, hidden, dnsend,
     dnx, dny, sx, sy, dn2x, dn2y,
     unitb, ubuf, gbuf, att, zbuf, tsend, trecv, gpb, tgb, g1, r1, g2, r2, g3, r3, g4s, g4r,
     lx, lt, lz, cz, send_sem, recv_sem,
@@ -183,9 +183,10 @@
     for d in (1, 2, 7, 6, 3, 5, 4):
         t = lax.rem(tp + d, 8)
         send(ctx.at[t], ctxp.at[tp, xy], "ctx", tp, t, dp)
-    selects = [select_units(q) for q in range(4)]
-    up = [dot_nt(selects[q], wu[...]) for q in range(4)]
-    down = [dot_nt(selects[q], wd[...]) for q in range(4)]
+    selects = [select_units(q) for q in range(3)]
+    unused = [jnp.zeros((128, 32), F32)]
+    up = [dot_nt(selects[q], wu[...]) for q in range(3)] + unused
+    down = [dot_nt(selects[q], wd[...]) for q in range(3)] + unused
     sp[:, 0:8] = jnp.concatenate(up, axis=1).reshape(16, 8, 128).astype(BF16)
     sp[:, 8:16] = jnp.concatenate(down, axis=1).reshape(16, 8, 128).astype(BF16)
     srecv[xy] = sp[xy]
@@ -231,15 +232,15 @@
     from_plane(srecv, "sp")
     for t in range(4):
         pieces = [srecv[4 * t + g].astype(F32) for g in range(4)]
-        for q in range(4):
+        for q in range(3):
             tile = jnp.zeros((16, 128), F32)
             for g in range(4):
                 shift = ((g - q) * 32) % 128
                 moved = pltpu.roll(pieces[g], shift, 1) if shift else pieces[g]
                 tile = jnp.where(group == g, moved, tile)
             hidden[8 * q : 8 * q + 8, 128 * t : 128 * t + 128] = tile[0:8]
-            hidden[32 + 8 * q : 40 + 8 * q, 128 * t : 128 * t + 128] = tile[8:16]
-    s4[c, zh, zl] = hidden[0:64, 0:512].astype(BF16)
+            hidden[24 + 8 * q : 32 + 8 * q, 128 * t : 128 * t + 128] = tile[8:16]
+    s4[c, zh, zl] = hidden[0:48, 0:512].astype(BF16)
     ring_start(1)
 
     ctx_own(0)
@@ -268,10 +269,10 @@
     k0 = math.sqrt(2.0 / math.pi)
 
     def up_part(zb):
-        return s4[:, :, zb, 0:32, :].reshape(256, 512)
+        return upw[:, 512 * zb : 512 * zb + 512]
 
     def down_part(zb):
-        return s4[:, :, zb, 32:64, :].reshape(256, 512)
+        return dnw[:, 512 * zb : 512 * zb + 512]
 
     def student(block):
         rs = slice(256 * block, 256 * block + 256)
@@ -339,6 +340,10 @@
     ring_step(1, 8)
     ring_step(0, 8)
     ring_last(1)
+    for zb in range(4):
+        whole = s4[:, :, zb].astype(F32)
+        upw[:, 512 * zb : 512 * zb + 512] = whole[:, :, 0:24].reshape(192, 512).astype(BF16)
+        dnw[:, 512 * zb : 512 * zb + 512] = whole[:, :, 24:48].reshape(192, 512).astype(BF16)
     student(0)
     student(1)
     for d in (1, 3, 2):
@@ -471,7 +476,7 @@
 
     def both_cores(zb):
         arrived(r1.at[zb], "g1", zb)
-        g2[zb] = (g1[zb, c] + r1[zb]).astype(BF16)
+        g2[zb] = (g1[zb, c] + r1[zb]).reshape(96, 512).astype(BF16)
         if zb is not zl:
             send(g2.at[zb], r2.at[zl], "g2", zl, tp, xy * 4 + zb)
 
@@ -479,7 +484,7 @@
     for d in (2, 1, 3, 0):
         zb = other(zl, d) if d else zl
         columns = pl.ds(pl.multiple_of(zb * 512, 512), 512)
-        g1[zb] = dot_tn(grad_pre, lifted[:, columns]).reshape(2, 4, 32, 512)
+        g1[zb] = dot_tn(grad_pre, lifted[:, columns]).reshape(2, 4, 24, 512)
         send(g1.at[zb, 1 - c], r1.at[zb], "g1", zb, sibling, dp)
         if previous is not None:
             both_cores(previous)
@@ -496,7 +501,9 @@
     for d in (1, 2, 3):
         zo = other(zl, d)
         arrived(r2.at[zo], "g2", zo)
-    g3[...] = (r2[0].astype(F32) + r2[1].astype(F32) + r2[2].astype(F32) + r2[3].astype(F32)).astype(BF16)
+    part = r2[0].astype(F32) + r2[1].astype(F32) + r2[2].astype(F32) + r2[3].astype(F32)
+    part = jnp.concatenate([part.reshape(4, 24, 512), jnp.zeros((4, 8, 512), F32)], axis=1)
+    g3[...] = part.astype(BF16)
     r3[zh] = g3[zh]
     for d in (1, 2, 3):
         ho = other(zh, d)
@@ -518,7 +525,7 @@
     for t in range(4):
         for g in range(4):
             tile = jnp.zeros((8, 128), F32)
-            for q in range(4):
+            for q in range(3):
                 shift = ((q - g) * 32) % 128
                 piece = total[8 * q : 8 * q + 8, 128 * t : 128 * t + 128]
                 moved = pltpu.roll(piece, shift, 1) if shift else piece
@@ -541,7 +548,7 @@
     middle = part.astype(BF16)
     low = (part - middle.astype(F32)).astype(BF16)
     grad = jnp.zeros((32, 384), F32)
-    for q in range(4):
+    for q in range(3):
         chosen = dot_tn(high, selects[q]) + dot_tn(middle, selects[q]) + dot_tn(low, selects[q])
         grad = grad + chosen[32 * q : 32 * q + 32]
     grad_out[...] = grad
@@ -554,7 +561,7 @@
     row = lax.broadcasted_iota(jnp.int32, (128, 384), 0)
     unit = lax.broadcasted_iota(jnp.int32, (128, 384), 1)
     r = lax.rem(row, 8)
-    chosen = (unit == lax.div(row, 8) * 24 + q * 6 + r) & (r < 6)
+    chosen = unit == lax.div(row, 8) * 24 + q * 8 + r
     return jnp.where(chosen, 1.0, 0.0).astype(BF16)
 
 
@@ -586,7 +593,9 @@
         scratch_shapes=[
             V((8, 16, 32, 512), BF16),
             V((8, 4, 64, 512), BF16),
-            V((2, 4, 4, 64, 512), BF16),
+            V((2, 4, 4, 48, 512), BF16),
+            V((192, 2048), BF16),
+            V((192, 2048), BF16),
             V((16, 16, 128), BF16),
             V((16, 16, 128), BF16),
             V((16, 32, 256), BF16),
@@ -596,7 +605,7 @@
             V((4, 16, 32, 128), BF16),
             V((256, 2048), BF16),
             V((512, 2048), BF16),
-            V((512, 256), F32),
+            V((512, 192), F32),
             V((64, 512), F32),
             V((4, 4, 32, 2048), BF16),
             V((4, 4, 32, 1024), BF16),
@@ -606,18 +615,18 @@
             V((4, 32, 1024), BF16),
             V((4, 32, 1024), BF16),
             V((16, 32, 2048), BF16),
-            V((512, 256), F32),
-            V((256, 128), BF16),
+            V((512, 192), F32),
+            V((192, 128), BF16),
             V((512, 256), F32),
             V((16, 32, 256), BF16),
             V((16, 72, 128), F32),
             V((16, 72, 128), F32),
             V((16, 32, 256), BF16),
             V((8, 32, 128), F32),
-            V((4, 2, 4, 32, 512), F32),
-            V((4, 4, 32, 512), F32),
-            V((4, 4, 32, 512), BF16),
-            V((4, 4, 32, 512), BF16),
+            V((4, 2, 4, 24, 512), F32),
+            V((4, 4, 24, 512), F32),
+            V((4, 96, 512), BF16),
+            V((4, 96, 512), BF16),
             V((4, 32, 512), BF16),
             V((4, 32, 512), BF16),
             V((16, 8, 128), F32),

time: 160 us -> 156 us (0.975)
  Pallas kernels: 152 us -> 149 us
    pallas_call x1, Pallas kernels: 152 us -> 149 us  [call(): pl.pallas_call(body, out_shape=(jax.ShapeDtypeStruct((8, 32, 128), F32),...]
where the time goes in v4:
time: 156 us
  Pallas kernels  149 us (96%)
  local copies, waits for them, and re-layouts  4.25 us (3%)
  between operations  2.1 us (1%)
    pallas_call x1, Pallas kernels, call(): pl.pallas_call(body, out_shape=(jax.ShapeDtypeStruct((8, 32, 128), F32),...  149 us

profile of v4, /device:TPU:32, one launch (start us, length us, event | category | flops | bytes accessed | tf_op | source)
XLA Modules:
  0.0 155.9 jit_solution(10683161139727161506)
XLA Ops:
  2.1 0.1 pad_maximum_fusion
  2.2 0.1 pad.2.clone
  2.3 0.1 maximum_convert_fusion
  2.4 0.7 maximum_maximum_fusion.info
  3.0 148.7 %shard_map.148 = (f32[8,32,128]{2,1,0:T(8,128)}, f32[32,384]{1,0:T(8,128)}, f32[8,128]{1,0:T(8,128)}) custom-call(bf16[8,32,512]{2,1,0:T(8,128)(2,1)} %bitcast.12, bf16[64,512]{1,0:T(8,128)(2,1)} %bitcast.14, bf16[32,384]{1,0:T(8,128)(2,1)} %wu.1, bf16[32,384]{1,0:T(8,128)(2,1)} %bitcast.17, bf16[256,4096]{1,0:T(8,128)(2,1)} %stream.1, ...), custom_call_target="tpu_custom_call" | custom-call | tf_op jit(solution)/shard_map/pallas_call | solution.py:584
  151.7 1.2 slice.3
  152.9 1.6 %copy.20 = f32[256,128]{1,0:T(8,128)} copy(f32[256,128]{1,0:T(8,128)} %bitcast.13) | data formatting | bytes 262144
  154.5 1.4 copy.21
  (2 shorter events, 0.1 us)
